TPU v7x, 32 devices: a whole 2x2x4 slice. The times are simulated.
32 devices in a mesh: groups: 2 (over y), tensor: 4 (over x, core), dp: 4 (over z).
Axes of the slice: x: 2, y: 2, z: 4, core: 2. Of those that a mesh axis runs over, the one named last changes fastest.
Arguments:
- activations: bfloat16 [8, 512, 4096], P(('groups', 'dp'), 'tensor'), parts along dimension 0, may hold values from -6 to 6
- out_grads: bfloat16 [8, 512, 14336], P(('groups', 'dp'), None, 'tensor'), parts along dimension 0, may hold values from -1 to 1
- q_start: bfloat16 [28672, 64], P(('groups', 'tensor')), parts along dimension 0, may hold values from -0.046875 to 0.046875
Outputs:
- weight_update: bfloat16 [8192, 14336], P(('groups', 'dp'), 'tensor'), parts along dimension 0
- q_new: float32 [28672, 64], P(('groups', 'tensor')), parts along dimension 0
- new_error: bfloat16 [8, 4096, 14336], P(('groups', 'dp'), None, 'tensor'), parts along dimension 0
There are 2 independent parts, one for each index of `groups`. A program takes and returns all parts, laid end to end along the dimension named above; each array names one. Nothing has to cross between parts.
All inputs are finite; a program needn't handle non-finite values.
Results may differ from a plain program's by a relative error of at most 0.0057.
Values may be sent and summed in bfloat16 or wider, within the bound.
A program may use at most 192 MiB of HBM per device.

v0:
```python
import jax
import jax.numpy as jnp
from jax import lax
from jax.sharding import PartitionSpec as P


def orthogonal(p_rows, gram_matrix):
    factor = jnp.linalg.cholesky(gram_matrix)
    return jax.scipy.linalg.solve_triangular(factor, p_rows.T, lower=True).T


def per_device(activations, out_grads, q_start):
    replicas = lax.axis_size("dp")
    gathered_rows = lax.all_gather(activations[0], "tensor", axis=0, tiled=True)
    weight_grad = lax.dot_general(
        gathered_rows, out_grads[0], (((0,), (0,)), ((), ())), preferred_element_type=jnp.float32
    )
    merged = weight_grad.astype(jnp.bfloat16)
    feature_count = merged.shape[0]
    p_term = jnp.dot(merged, q_start, preferred_element_type=jnp.float32)
    p_avg = lax.psum(p_term, ("tensor", "dp")) / replicas
    gram_matrix = jnp.dot(p_avg.T, p_avg, precision=lax.Precision.HIGHEST)
    p_orth = orthogonal(p_avg, gram_matrix)
    p_low = p_orth.astype(jnp.bfloat16)
    q_term = lax.dot_general(
        merged, p_low, (((0,), (0,)), ((), ())), preferred_element_type=jnp.float32
    )
    q_new = lax.psum(q_term, "dp") / replicas
    decompressed = jnp.dot(p_orth, q_new.T, precision=lax.Precision.HIGHEST)
    block_rows = feature_count // replicas
    own_rows = lax.dynamic_slice_in_dim(
        decompressed, lax.axis_index("dp") * block_rows, block_rows, 0
    )
    weight_update = own_rows.astype(jnp.bfloat16)
    new_error = (merged.astype(jnp.float32) - decompressed).astype(jnp.bfloat16)[None]
    return (weight_update, q_new, new_error)


def solution(mesh):
    return jax.shard_map(
        per_device,
        mesh=mesh,
        in_specs=(
            P(("groups", "dp"), "tensor", None),
            P(("groups", "dp"), None, "tensor"),
            P(("groups", "tensor"), None),
        ),
        out_specs=(
            P(("groups", "dp"), "tensor"),
            P(("groups", "tensor"), None),
            P(("groups", "dp"), None, "tensor"),
        ),
        check_vma=False,
    )
```

profile of v0, /device:TPU:0, one launch (start us, length us, event | category | flops | bytes accessed | tf_op | source)
XLA Modules:
  0.0 360.7 jit_solution(250885951957382663)
XLA Ops:
  7.2 0.0 copy-start
  7.2 0.0 all-gather.3.cloned.1.call-start
  7.2 0.7 all-gather.3.cloned.1.call-update
  7.9 0.0 all-reduce.3.cloned.1.call-start
  8.0 38.8 %all-gather.3.cloned.1.call-done = bf16[1,512,4096]{2,1,0:T(8,128)(2,1)} async-done(((bf16[1,128,4096]{2,1,0:T(8,128)(2,1)}), bf16[1,512,4096]{2,1,0:T(8,128)(2,1)}) %all-gather.3.cloned.1.call-update) | async-done | bytes 4194320 | tf_op jit(solution)/shard_map/all_gather | solution.py:14
  46.8 22.5 %convolution_convert_fusion = bf16[4096,3584]{1,0:T(8,128)(2,1)} fusion(bf16[1,512,4096]{2,1,0:T(8,128)(2,1)} %all-gather.3.cloned.1.call-done, bf16[1,512,3584]{2,1,0:T(8,128)(2,1)} %param.4), kind=kOutput, calls=%fused_computation.1 | convolution fusion | flops 15047065600 | bytes 37224448 | tf_op jit(solution)/shard_map/dot_general | solution.py:15
  69.3 0.0 copy-done
  69.3 15.2 %fusion.16 = f32[4096,64]{0,1:T(8,128)} fusion(bf16[4096,3584]{1,0:T(8,128)(2,1)} %convolution_convert_fusion, bf16[3584,64]{0,1:T(8,128)(2,1)S(1)} %copy-done), kind=kOutput, calls=%fused_computation.26 | convolution fusion | flops 1879048192 | bytes 30867456 | tf_op jit(solution)/shard_map/dot_general | solution.py:20
  84.5 0.0 all-reduce.3.cloned.1.call-update
  84.5 0.0 all-reduce.5.cloned.1.call-start
  84.6 93.4 %all-reduce.3.cloned.1.call-done = f32[4096,64]{0,1:T(8,128)} async-done(((f32[4096,64]{0,1:T(8,128)}), f32[4096,64]{0,1:T(8,128)}) %all-reduce.3.cloned.1.call-update) | async-done | bytes 1048592 | tf_op jit(solution)/shard_map/psum | solution.py:21
  178.0 2.6 fusion.5
  180.6 0.1 copy.6
  180.7 5.8 %cholesky.16 = f32[64,64]{1,0:T(8,128)S(1)} custom-call(f32[64,64]{1,0:T(8,128)S(1)} %fusion.13), custom_call_target="Cholesky" | custom-call | tf_op jit(solution)/shard_map/jit(cholesky)/cholesky | solution.py:8
  186.5 0.6 compare_reduce_fusion
  187.2 0.7 fusion.11
  187.8 4.9 %custom-call.7 = f32[1,64,64]{1,2,0:T(8,128)S(1)} custom-call(f32[1,64,64]{2,1,0:T(8,128)S(1)} %fusion.11), custom_call_target="InvertDiagBlocksLowerTriangular" | custom-call | tf_op jit(solution)/shard_map/jit(_solve_triangular)/triangular_solve | solution.py:9
  192.7 2.3 fusion.3
  195.0 13.1 %fusion.7 = f32[3584,64]{0,1:T(8,128)} fusion(bf16[4096,3584]{1,0:T(8,128)(2,1)} %convolution_convert_fusion, f32[64,4096]{1,0:T(8,128)S(1)} %fusion.3), kind=kOutput, calls=%fused_computation.10 | convolution fusion | flops 1879310336 | bytes 31326208 | tf_op jit(solution)/shard_map/dot_general | solution.py:25
  208.1 0.0 all-reduce.5.cloned.1.call-update
  208.1 47.2 %all-reduce.5.cloned.1.call-done = f32[3584,64]{0,1:T(8,128)} async-done(((f32[3584,64]{0,1:T(8,128)}), f32[3584,64]{0,1:T(8,128)}) %all-reduce.5.cloned.1.call-update) | async-done | bytes 917520 | tf_op jit(solution)/shard_map/psum | solution.py:28
  255.3 1.2 broadcast_multiply_fusion
  256.5 0.0 copy-start.2
  256.5 50.5 %fusion.17 = f32[4096,3584]{1,0:T(8,128)} fusion(f32[64,4096]{1,0:T(8,128)S(1)} %fusion.3, f32[3584,64]{0,1:T(8,128)S(1)} %broadcast_multiply_fusion), kind=kOutput, calls=%fused_computation.27 | convolution fusion | flops 11274289152 | bytes 60686336 | tf_op jit(solution)/shard_map/dot_general | solution.py:29
  307.0 0.0 copy-done.2
  307.0 0.0 copy-start.1
  307.0 38.0 %fusion = bf16[1,4096,3584]{2,1,0:T(8,128)(2,1)} fusion(f32[4096,3584]{1,0:T(8,128)} %fusion.17, bf16[4096,3584]{1,0:T(8,128)(2,1)} %convolution_convert_fusion), kind=kLoop, calls=%fused_computation.2 | loop fusion | flops 44040192 | bytes 117440512 | tf_op jit(solution)/shard_map/broadcast_in_dim | solution.py:35
  345.0 9.1 %dynamic-slice_convert_fusion = bf16[1024,3584]{1,0:T(8,128)(2,1)} fusion(f32[4096,3584]{1,0:T(8,128)} %fusion.17, s32[]{:T(128)S(6)} %select_n.8), kind=kLoop, calls=%fused_computation.3 | loop fusion | bytes 14680068 | tf_op jit(solution)/shard_map/convert_element_type | solution.py:34
  354.1 0.0 copy-done.1
  (2 shorter events, 0.0 us)
Async XLA Ops:
  7.2 62.1 %copy-start = (bf16[3584,64]{0,1:T(8,128)(2,1)S(1)}, bf16[3584,64]{0,1:T(8,128)(2,1)}, u32[]{:S(2)}) copy-start(bf16[3584,64]{0,1:T(8,128)(2,1)} %param.5) | copy-start | bytes 1376260
  7.2 39.6 %all-gather.3.cloned.1.call-start = ((), (), s32[]{:S(2)}) async-start(), calls=%async_computation.2 | async-start | bytes 5242880 | tf_op jit(solution)/shard_map/all_gather | solution.py:14
  7.9 170.1 %all-reduce.3.cloned.1.call-start = ((), (), s32[]{:S(2)}) async-start(), calls=%async_computation | async-start | bytes 2097152 | tf_op jit(solution)/shard_map/psum | solution.py:21
  84.5 170.8 %all-reduce.5.cloned.1.call-start = ((), (), s32[]{:S(2)}) async-start(), calls=%async_computation.1 | async-start | bytes 1835008 | tf_op jit(solution)/shard_map/psum | solution.py:28
  256.5 50.5 %copy-start.2 = (f32[3584,64]{0,1:T(8,128)}, f32[3584,64]{0,1:T(8,128)S(1)}, u32[]{:S(2)}) copy-start(f32[3584,64]{0,1:T(8,128)S(1)} %broadcast_multiply_fusion) | copy-start | bytes 2752516
  307.0 47.1 %copy-start.1 = (bf16[3584,64]{0,1:T(8,128)(2,1)S(1)}, bf16[3584,64]{0,1:T(8,128)(2,1)}, u32[]{:S(2)}) copy-start(bf16[3584,64]{0,1:T(8,128)(2,1)} %param.5) | copy-start | bytes 1376260
Sparse Core Ops, SparseCore 0:
  9.6 37.1 all-gather.2
  84.6 93.3 all-reduce.2
  208.2 46.9 all-reduce.4
where the time goes:
time: 361 us
  waiting for transfers between devices  180 us (50%)
  matrix products  106 us (29%)
  other arithmetic  51.3 us (14%)
  between operations  13.8 us (4%)
  local copies, waits for them, and re-layouts  9.19 us (3%)
    psum x1, waiting for transfers between devices, per_device(): p_avg = lax.psum(p_term, ('tensor', 'dp')) / replicas  93.4 us
    dot_general x1, matrix products, per_device(): decompressed = jnp.dot(p_orth, q_new.T, precision=lax.Precision.HIGHEST)  50.5 us
    psum x1, waiting for transfers between devices, per_device(): q_new = lax.psum(q_term, 'dp') / replicas  47.2 us
    all_gather x1, waiting for transfers between devices, per_device(): gathered_rows = lax.all_gather(activations[0], 'tensor', axis=0, tiled=True)  38.8 us
    broadcast_in_dim x1, other arithmetic, per_device(): (merged.astype(jnp.float32) - decompressed).astype(jnp.bfloat16)[None]  38 us
    dot_general x1, matrix products, per_device(): lax.dot_general(gathered_rows, out_grads[0], (((0,), (0,)), ((), ())), pr...  22.5 us
    dot_general x1, matrix products, per_device(): p_term = jnp.dot(merged, q_start, preferred_element_type=jnp.float32)  15.2 us
    dot_general x1, matrix products, per_device(): lax.dot_general(merged, p_low, (((0,), (0,)), ((), ())), preferred_elemen...  13.1 us
  transfers between devices with their start and end apart: 3, of which 3 were waited for; matrix products, arithmetic and copies ran while one was open for 0% of the time, Pallas kernels for 0%

commit v1 on v0

v1 whole, which is shorter than its diff:
```python
import functools

import jax
import jax.numpy as jnp
from jax import lax
from jax.experimental import pallas as pl
from jax.experimental.pallas import tpu as pltpu
from jax.sharding import PartitionSpec as P

MESH = pl.DeviceIdType.MESH
HIGHEST = lax.Precision.HIGHEST
F32 = jnp.float32
BF16 = jnp.bfloat16


def dot(a, b, dims, precision=None):
    return lax.dot_general(
        a, b, (dims, ((), ())), precision=precision, preferred_element_type=F32
    )


def split(x):
    high = x.astype(BF16)
    return high, (x - high.astype(F32)).astype(BF16)


def inverse_factor(gram):
    rank = gram.shape[0]
    shape = (rank, 2 * rank)
    rows = lax.broadcasted_iota(jnp.int32, shape, 0)
    lanes = lax.broadcasted_iota(jnp.int32, shape, 1)
    eye = (lanes == rows + rank).astype(F32)
    wide = jnp.concatenate([gram, jnp.zeros_like(gram)], axis=1) + eye
    done = []
    for k in range(rank):
        top = (k // 8) * 8
        here = k - top
        column = jnp.broadcast_to(wide[:, k : k + 1], wide.shape)
        pivot_row = wide[here : here + 1, :]
        pivot = column[here : here + 1, :]
        done.append(pivot_row * lax.rsqrt(pivot))
        if k == rank - 1:
            break
        scaled = pivot_row / pivot
        below = lax.broadcasted_iota(jnp.int32, wide.shape, 0) > here
        wide = jnp.where(below, wide - column * scaled, wide)
        if here == 7:
            wide = wide[8:, :]
    return jnp.concatenate(done, axis=0)[:, rank:]


def factors_kernel(
    nt, nd, a_ref, g_ref, q_ref, acat_ref, qnew_ref,
    a_buf, g_buf, q_buf, h_loc, h_sib, h_chip, h_x, p_part, p_recv, p_all, p_t, p_neg,
    q_f32, q_part, q_recv, q_all,
    local_sems, a_sib_sems, a_x_sems, a_fwd_sems, h_sib_sems, h_x_sems,
    prs_sems, pag_sems, psib_sems, px_sems, pfwd_sems, qrs_sems, qag_sems,
):
    nx = nt // 2
    t, z = lax.axis_index("tensor"), lax.axis_index("dp")
    chip, core = t // 2, t % 2
    sibling = chip * 2 + 1 - core
    tok, depth = a_ref.shape[1], a_ref.shape[2]
    tokens = nt * tok
    rank = q_ref.shape[1]
    part = depth // nt
    chunk = part // nd
    q_rows = rank // nd
    pieces = a_x_sems.shape[2]
    piece = tok // pieces
    pending = []

    def x_peer(d):
        return lax.rem(chip + d, nx) * 2 + core

    def x_source(d):
        return lax.rem(chip + nx - d, nx) * 2 + core

    def z_peer(d):
        return lax.rem(z + d, nd)

    def z_source(d):
        return lax.rem(z + nd - d, nd)

    def send(src, dst, sems, axis, peer):
        copy = pltpu.make_async_remote_copy(
            src_ref=src, dst_ref=dst, send_sem=sems.at[0], recv_sem=sems.at[1],
            device_id={axis: peer}, device_id_type=MESH,
        )
        copy.start()
        pending.append(copy)
        return copy

    def token_rows(block, p):
        return pl.ds(pl.multiple_of(block * tok + p * piece, piece), piece)

    loads = [
        pltpu.make_async_copy(g_ref.at[0], g_buf, local_sems.at[0]),
        pltpu.make_async_copy(q_ref, q_buf, local_sems.at[1]),
        pltpu.make_async_copy(
            a_ref.at[0], a_buf.at[pl.ds(pl.multiple_of(t * tok, tok), tok)], local_sems.at[2]
        ),
    ]
    for load in loads:
        load.start()

    barrier = pltpu.get_barrier_semaphore()
    for d in range(1, nt):
        pl.semaphore_signal(
            barrier, inc=1, device_id={"tensor": lax.rem(t + d, nt)}, device_id_type=MESH
        )
    for d in range(1, nd):
        pl.semaphore_signal(barrier, inc=1, device_id={"dp": z_peer(d)}, device_id_type=MESH)
    pl.semaphore_wait(barrier, nt - 1 + nd - 1)

    a_x = {}
    for p in range(pieces):
        for d in range(1, nx):
            a_x[d, p] = send(
                a_ref.at[0, pl.ds(p * piece, piece)], a_buf.at[token_rows(t, p)],
                a_x_sems.at[d, :, p], "tensor", x_peer(d),
            )
    a_sib = send(
        a_ref.at[0], a_buf.at[pl.ds(pl.multiple_of(t * tok, tok), tok)],
        a_sib_sems, "tensor", sibling,
    )

    loads[0].wait()
    loads[1].wait()
    h_loc[...] = dot(g_buf[...], q_buf[...], ((1,), (0,))).T
    h_sib_copy = send(h_loc, h_sib, h_sib_sems, "tensor", sibling)
    h_sib_copy.wait_recv()
    h_chip[...] = h_loc[...] + h_sib[...]
    h_copies = [
        send(h_chip, h_x.at[d], h_x_sems.at[d], "tensor", x_peer(d)) for d in range(1, nx)
    ]

    a_fwd = []
    for p in range(pieces):
        for d in range(1, nx):
            a_x[d, p].wait_recv()
            rows = token_rows(x_source(d), p)
            a_fwd.append(
                send(a_buf.at[rows], a_buf.at[rows], a_fwd_sems.at[d, :, p], "tensor", sibling)
            )
    h_sum = h_chip[...]
    for d, copy in zip(range(1, nx), h_copies):
        copy.wait_recv()
        h_sum = h_sum + h_x[d]
    loads[2].wait()
    a_sib.wait_recv()
    for copy in a_fwd:
        copy.wait_recv()
    a_out = pltpu.make_async_copy(a_buf, acat_ref.at[pl.ds(0, tokens)], local_sems.at[3])
    a_out.start()

    h_both = jnp.concatenate(split(h_sum), axis=0)
    own = dot(
        h_both, a_buf[:, pl.ds(pl.multiple_of(t * part, part), part)], ((1,), (0,))
    )
    own = (own[:rank] + own[rank:]) * (1.0 / nd)
    for j in range(nd):
        p_part[j] = own[:, j * chunk : (j + 1) * chunk]
    copies = [
        send(p_part.at[z_peer(d)], p_recv.at[d], prs_sems.at[d], "dp", z_peer(d))
        for d in range(1, nd)
    ]
    total = p_part[z]
    for d, copy in zip(range(1, nd), copies):
        copy.wait_recv()
        total = total + p_recv[d]
    p_all[t, z] = total
    pag = [None] + [
        send(p_all.at[t, z], p_all.at[t, z], pag_sems.at[d], "dp", z_peer(d))
        for d in range(1, nd)
    ]
    psib, px, pfwd = [], {}, []
    for d in range(nd):
        if d:
            pag[d].wait_recv()
        block = p_all.at[t, z_source(d)]
        for e in range(1, nx):
            px[e, d] = send(block, block, px_sems.at[e, :, d], "tensor", x_peer(e))
        psib.append(send(block, block, psib_sems.at[:, d], "tensor", sibling))
    for d in range(nd):
        for e in range(1, nx):
            px[e, d].wait_recv()
            block = p_all.at[x_source(e), z_source(d)]
            pfwd.append(send(block, block, pfwd_sems.at[e, :, d], "tensor", sibling))
    for copy in psib + pfwd:
        copy.wait_recv()
    for i in range(nt):
        for j in range(nd):
            start = i * part + j * chunk
            p_t[:, start : start + chunk] = p_all[i, j]

    gram = dot(p_t[...], p_t[...], ((1,), (1,)), HIGHEST)
    inverse = inverse_factor(gram)
    p_orth = dot(inverse, p_t[...], ((1,), (0,)), HIGHEST)
    p_high, p_rest = split(p_orth)
    p_neg[0:rank] = -p_high
    p_neg[rank : 2 * rank] = -p_rest
    p_out = pltpu.make_async_copy(
        p_neg, acat_ref.at[pl.ds(tokens, 2 * rank)], local_sems.at[4]
    )
    p_out.start()

    u_both = jnp.concatenate(split(dot(p_high, a_buf[...], ((1,), (1,)))), axis=0)
    term = dot(u_both, g_buf[...], ((1,), (0,)))
    term = (term[:rank] + term[rank:]) * (1.0 / nd)
    q_f32[...] = term
    for j in range(nd):
        q_part[j] = term[j * q_rows : (j + 1) * q_rows].astype(q_part.dtype)
    copies = [
        send(q_part.at[z_peer(d)], q_recv.at[d], qrs_sems.at[d], "dp", z_peer(d))
        for d in range(1, nd)
    ]
    total = q_f32[pl.ds(pl.multiple_of(z * q_rows, q_rows), q_rows), :]
    for d, copy in zip(range(1, nd), copies):
        copy.wait_recv()
        total = total + q_recv[d].astype(F32)
    q_all[z] = total.astype(q_all.dtype)
    copies = [
        send(q_all.at[z], q_all.at[z], qag_sems.at[d], "dp", z_peer(d)) for d in range(1, nd)
    ]
    for copy in copies:
        copy.wait_recv()
    q_out = pltpu.make_async_copy(q_all, qnew_ref, local_sems.at[5])
    q_out.start()
    for copy in pending:
        copy.wait_send()
    a_out.wait()
    p_out.wait()
    q_out.wait()


def factors(nt, nd, activations, out_grads, q_start):
    tok, depth = activations.shape[1:]
    tokens, width = out_grads.shape[1:]
    rank = q_start.shape[1]
    nx = nt // 2
    pieces = 2
    part = depth // nt
    chunk = part // nd
    q_rows = rank // nd
    q_type = BF16 if q_rows % 16 == 0 else F32
    dma = pltpu.SemaphoreType.DMA
    anywhere = pl.BlockSpec(memory_space=pl.ANY)
    return pl.pallas_call(
        functools.partial(factors_kernel, nt, nd),
        out_shape=(
            jax.ShapeDtypeStruct((tokens + 2 * rank, depth), BF16),
            jax.ShapeDtypeStruct((nd, q_rows, width), q_type),
        ),
        in_specs=[anywhere] * 3,
        out_specs=(anywhere, anywhere),
        scratch_shapes=[
            pltpu.VMEM((tokens, depth), BF16),
            pltpu.VMEM((tokens, width), BF16),
            pltpu.VMEM((width, rank), BF16),
            pltpu.VMEM((rank, tokens), F32),
            pltpu.VMEM((rank, tokens), F32),
            pltpu.VMEM((rank, tokens), F32),
            pltpu.VMEM((nx, rank, tokens), F32),
            pltpu.VMEM((nd, rank, chunk), F32),
            pltpu.VMEM((nd, rank, chunk), F32),
            pltpu.VMEM((nt, nd, rank, chunk), F32),
            pltpu.VMEM((rank, depth), F32),
            pltpu.VMEM((2 * rank, depth), BF16),
            pltpu.VMEM((rank, width), F32),
            pltpu.VMEM((nd, q_rows, width), q_type),
            pltpu.VMEM((nd, q_rows, width), q_type),
            pltpu.VMEM((nd, q_rows, width), q_type),
            dma((6,)),
            dma((2,)),
            dma((nx, 2, pieces)),
            dma((nx, 2, pieces)),
            dma((2,)),
            dma((nx, 2)),
            dma((nd, 2)),
            dma((nd, 2)),
            dma((2, nd)),
            dma((nx, 2, nd)),
            dma((nx, 2, nd)),
            dma((nd, 2)),
            dma((nd, 2)),
        ],
        compiler_params=pltpu.CompilerParams(
            collective_id=0, has_side_effects=True, vmem_limit_bytes=48 * 2**20
        ),
        name="factors",
    )(activations, out_grads, q_start)


def finish_kernel(own, z_ref, acat_ref, g_ref, q_ref, wu_ref, qnew_ref, err_ref, lhs, both):
    step = pl.program_id(0)
    tokens, width = g_ref.shape[1:]
    rank = q_ref.shape[0]
    lhs[...] = acat_ref[...].T

    @pl.when(step == 0)
    def _():
        both[0:rank] = q_ref[...].astype(BF16)
        both[rank : 2 * rank] = q_ref[...].astype(BF16)
        qnew_ref[...] = q_ref[...].astype(F32).T

    columns = 512 if width % 512 == 0 else 128
    for j in range(width // columns):
        cols = slice(j * columns, (j + 1) * columns)
        minus = dot(lhs[:, tokens:], both[:, cols], ((1,), (0,)))
        err_ref[0, :, cols] = (
            dot(lhs[:, :tokens], g_ref[0, :, cols], ((1,), (0,))) + minus
        ).astype(BF16)

    @pl.when(step < own)
    def _():
        for j in range(width // columns):
            cols = slice(j * columns, (j + 1) * columns)
            minus = dot(lhs[:, tokens:], both[:, cols], ((1,), (0,)))
            wu_ref[:, cols] = (-minus).astype(BF16)


def finish(nd, acat, out_grads, q_t):
    depth = acat.shape[1]
    tokens, width = out_grads.shape[1:]
    rank = q_t.shape[0]
    rows = 256
    steps = depth // rows
    own = steps // nd

    def at(i, z):
        return lax.rem(i + z[0] * own, steps)

    z = lax.axis_index("dp").astype(jnp.int32).reshape(1)
    return pl.pallas_call(
        functools.partial(finish_kernel, own),
        out_shape=(
            jax.ShapeDtypeStruct((depth // nd, width), BF16),
            jax.ShapeDtypeStruct((width, rank), F32),
            jax.ShapeDtypeStruct((1, depth, width), BF16),
        ),
        grid_spec=pltpu.PrefetchScalarGridSpec(
            num_scalar_prefetch=1,
            grid=(steps,),
            in_specs=[
                pl.BlockSpec((acat.shape[0], rows), lambda i, z: (0, at(i, z))),
                pl.BlockSpec((1, tokens, width), lambda i, z: (0, 0, 0)),
                pl.BlockSpec((rank, width), lambda i, z: (0, 0)),
            ],
            out_specs=(
                pl.BlockSpec((rows, width), lambda i, z: (jnp.minimum(i, own - 1), 0)),
                pl.BlockSpec((width, rank), lambda i, z: (0, 0)),
                pl.BlockSpec((1, rows, width), lambda i, z: (0, at(i, z), 0)),
            ),
            scratch_shapes=[
                pltpu.VMEM((rows, acat.shape[0]), BF16),
                pltpu.VMEM((2 * rank, width), BF16),
            ],
        ),
        compiler_params=pltpu.CompilerParams(
            dimension_semantics=("arbitrary",), vmem_limit_bytes=48 * 2**20
        ),
        name="finish",
    )(z, acat, out_grads, q_t)


def per_device(nt, nd, activations, out_grads, q_start):
    acat, q_parts = factors(nt, nd, activations, out_grads, q_start)
    q_t = q_parts.reshape(q_start.shape[1], out_grads.shape[2])
    return finish(nd, acat, out_grads, q_t)


def solution(mesh):
    return jax.shard_map(
        functools.partial(per_device, mesh.shape["tensor"], mesh.shape["dp"]),
        mesh=mesh,
        in_specs=(
            P(("groups", "dp"), "tensor", None),
            P(("groups", "dp"), None, "tensor"),
            P(("groups", "tensor"), None),
        ),
        out_specs=(
            P(("groups", "dp"), "tensor"),
            P(("groups", "tensor"), None),
            P(("groups", "dp"), None, "tensor"),
        ),
        check_vma=False,
    )
```

time: 361 us -> 125 us (0.35)
  waiting for transfers between devices: 180 us -> 0 us
  Pallas kernels: 0 us -> 115 us
  matrix products: 106 us -> 0 us
  other arithmetic: 51.3 us -> 0 us
  between operations: 13.8 us -> 0.67 us
    psum x2 -> x0, waiting for transfers between devices: 141 us -> none  [the longest x1 93.4 us: per_device(): p_avg = lax.psum(p_term, ('tensor', 'dp')) / replicas]
    pallas_call x0 -> x2, Pallas kernels: none -> 115 us  [the longest x1 81.6 us: factors(): pl.pallas_call(functools.partial(factors_kernel, nt, nd), out_shape=(jax....]
    dot_general x5 -> x0, matrix products: 104 us -> none  [the longest x1 50.5 us: per_device(): decompressed = jnp.dot(p_orth, q_new.T, precision=lax.Precision.HIGHEST)]
    all_gather x1 -> x0, waiting for transfers between devices: 38.8 us -> none  [per_device(): gathered_rows = lax.all_gather(activations[0], 'tensor', axis=0, tiled=True)]
    broadcast_in_dim x1 -> x0, other arithmetic: 38 us -> none  [per_device(): (merged.astype(jnp.float32) - decompressed).astype(jnp.bfloat16)[None]]
    another operation x5 -> x0, other arithmetic: 12.1 us -> none  [the longest x3 6.52 us: orthogonal(): factor = jnp.linalg.cholesky(gram_matrix)]
    convert_element_type x1 -> x0, local copies, waits for them, and re-layouts: 9.09 us -> none  [per_device(): weight_update = own_rows.astype(jnp.bfloat16)]
    unnamed x6 -> x7, local copies, waits for them, and re-layouts: 0.02 us -> 4.71 us
  transfers between devices with their start and end apart: 3 -> 0, of which waited for: 3 -> 0; matrix products, arithmetic and copies ran while one was open for 0% -> 0% of each run, Pallas kernels for 0% -> 0%
where the time goes in v1:
time: 125 us; the launch traced here: 122 us
  Pallas kernels  115 us (92%)
  local copies, waits for them, and re-layouts  6.15 us (5%)
    pallas_call x1, Pallas kernels, factors(): pl.pallas_call(functools.partial(factors_kernel, nt, nd), out_shape=(jax....  81.6 us
    pallas_call x1, Pallas kernels, finish(): pl.pallas_call(functools.partial(finish_kernel, own), out_shape=(jax.Shap...  33.7 us
    unnamed x7, local copies, waits for them, and re-layouts  4.71 us

profile of v1, /device:TPU:0, one launch (start us, length us, event | category | flops | bytes accessed | tf_op | source)
XLA Modules:
  0.0 122.1 jit_solution(2861555706328054382)
XLA Ops:
  0.6 1.4 %copy.6.q_ref = bf16[3584,64]{1,0:T(8,128)(2,1)S(1)} copy(bf16[3584,64]{0,1:T(8,128)(2,1)} %param.5) | data formatting | bytes 917504 | tf_op args[2]
  2.1 0.0 copy-start
  2.1 2.0 %copy-done = bf16[1,512,3584]{2,1,0:T(8,128)(2,1)S(1)} copy-done((bf16[1,512,3584]{2,1,0:T(8,128)(2,1)S(1)}, bf16[1,512,3584]{2,1,0:T(8,128)(2,1)}, u32[]{:S(2)}) %copy-start) | copy-done | bytes 3670040
  4.1 0.0 copy-start.2
  4.1 1.2 %copy-done.2 = bf16[1,128,4096]{2,1,0:T(8,128)(2,1)S(1)} copy-done((bf16[1,128,4096]{2,1,0:T(8,128)(2,1)S(1)}, bf16[1,128,4096]{2,1,0:T(8,128)(2,1)}, u32[]{:S(2)}) %copy-start.2) | copy-done | bytes 1048600
  5.4 0.0 copy-start.1
  5.4 81.6 %factors.1 = (bf16[640,4096]{1,0:T(8,128)(2,1)}, bf16[4,16,3584]{2,1,0:T(8,128)(2,1)S(1)}) custom-call(bf16[1,128,4096]{2,1,0:T(8,128)(2,1)S(1)} %copy-done.2, bf16[1,512,3584]{2,1,0:T(8,128)(2,1)S(1)} %copy-done, bf16[3584,64]{1,0:T(8,128)(2,1)S(1)} %copy.6.q_ref), custom_call_target="tpu_custom_call" | custom-call | tf_op jit(solution)/shard_map/factors/pallas_call | solution.py:249
  87.0 0.0 copy-done.1
  87.0 33.7 %finish.1 = (bf16[1024,3584]{1,0:T(8,128)(2,1)}, f32[3584,64]{1,0:T(8,128)S(1)}, bf16[1,4096,3584]{2,1,0:T(8,128)(2,1)}) custom-call(s32[1]{0:T(128)} %bitcast.z_ref, bf16[640,4096]{1,0:T(8,128)(2,1)} %get-tuple-element.5.acat_ref, bf16[1,512,3584]{2,1,0:T(8,128)(2,1)S(1)} %copy-done.1, bf16[64,3584]{1,0:T(8,128)(2,1)S(1)} %bitcast.2), custom_call_target="tpu_custom_call" | custom-call | tf_op jit(solution)/shard_map/finish/pallas_call | solution.py:335
  120.7 1.4 %copy.7 = f32[3584,64]{0,1:T(8,128)} copy(f32[3584,64]{1,0:T(8,128)S(1)} %get-tuple-element.8) | data formatting | bytes 1835008 | tf_op jit(solution)/shard_map/finish/pallas_call | solution.py:335
Async XLA Ops:
  2.1 2.0 %copy-start = (bf16[1,512,3584]{2,1,0:T(8,128)(2,1)S(1)}, bf16[1,512,3584]{2,1,0:T(8,128)(2,1)}, u32[]{:S(2)}) copy-start(bf16[1,512,3584]{2,1,0:T(8,128)(2,1)} %g_ref.3) | copy-start | bytes 11010052
  4.1 1.2 %copy-start.2 = (bf16[1,128,4096]{2,1,0:T(8,128)(2,1)S(1)}, bf16[1,128,4096]{2,1,0:T(8,128)(2,1)}, u32[]{:S(2)}) copy-start(bf16[1,128,4096]{2,1,0:T(8,128)(2,1)} %a_ref.1) | copy-start | bytes 3145732
  5.4 81.6 %copy-start.1 = (bf16[1,512,3584]{2,1,0:T(8,128)(2,1)S(1)}, bf16[1,512,3584]{2,1,0:T(8,128)(2,1)}, u32[]{:S(2)}) copy-start(bf16[1,512,3584]{2,1,0:T(8,128)(2,1)} %g_ref.3) | copy-start | bytes 11010052

commit v2 on v1

--- a/solution.py
+++ b/solution.py
@@ -50,11 +50,11 @@
 
 
 def factors_kernel(
-    nt, nd, a_ref, g_ref, q_ref, acat_ref, qnew_ref,
-    a_buf, g_buf, q_buf, h_loc, h_sib, h_chip, h_x, p_part, p_recv, p_all, p_t, p_neg,
-    q_f32, q_part, q_recv, q_all,
-    local_sems, a_sib_sems, a_x_sems, a_fwd_sems, h_sib_sems, h_x_sems,
-    prs_sems, pag_sems, psib_sems, px_sems, pfwd_sems, qrs_sems, qag_sems,
+    nt, nd, a_ref, g_ref, q_ref, merged_ref, pneg_ref, qnew_ref,
+    a_buf, g_buf, q_buf, h_loc, h_sib, h_chip, h_x, p_here, p_there, p_part, p_recv, p_all, p_t,
+    p_neg, q_f32, q_part, q_recv, q_all, stage,
+    local_sems, stage_sems, a_sib_sems, a_x_sems, a_fwd_sems, h_sib_sems, h_x_sems,
+    ptok_sems, prs_sems, pag_sems, psib_sems, px_sems, pfwd_sems, qrs_sems, qag_sems,
 ):
     nx = nt // 2
     t, z = lax.axis_index("tensor"), lax.axis_index("dp")
@@ -62,11 +62,13 @@
     sibling = chip * 2 + 1 - core
     tok, depth = a_ref.shape[1], a_ref.shape[2]
     tokens = nt * tok
-    rank = q_ref.shape[1]
+    rank = q_ref.shape[0]
     part = depth // nt
     chunk = part // nd
     q_rows = rank // nd
     pieces = a_x_sems.shape[2]
+    early = max(1, pieces // 4)
+    pair = 2 * tok
     piece = tok // pieces
     pending = []
 
@@ -113,58 +115,80 @@
         pl.semaphore_signal(barrier, inc=1, device_id={"dp": z_peer(d)}, device_id_type=MESH)
     pl.semaphore_wait(barrier, nt - 1 + nd - 1)
 
-    a_x = {}
-    for p in range(pieces):
-        for d in range(1, nx):
-            a_x[d, p] = send(
-                a_ref.at[0, pl.ds(p * piece, piece)], a_buf.at[token_rows(t, p)],
-                a_x_sems.at[d, :, p], "tensor", x_peer(d),
-            )
+    a_x, a_fwd = {}, []
+
+    def send_tokens(first, last):
+        for p in range(first, last):
+            for d in range(1, nx):
+                a_x[d, p] = send(
+                    a_ref.at[0, pl.ds(p * piece, piece)], a_buf.at[token_rows(t, p)],
+                    a_x_sems.at[d, :, p], "tensor", x_peer(d),
+                )
+
+    def forward_tokens(first, last):
+        for p in range(first, last):
+            for d in range(1, nx):
+                a_x[d, p].wait_recv()
+                rows = token_rows(x_source(d), p)
+                a_fwd.append(
+                    send(
+                        a_buf.at[rows], a_buf.at[rows], a_fwd_sems.at[d, :, p],
+                        "tensor", sibling,
+                    )
+                )
+
     a_sib = send(
         a_ref.at[0], a_buf.at[pl.ds(pl.multiple_of(t * tok, tok), tok)],
         a_sib_sems, "tensor", sibling,
     )
+    send_tokens(0, early)
 
     loads[0].wait()
     loads[1].wait()
-    h_loc[...] = dot(g_buf[...], q_buf[...], ((1,), (0,))).T
+    h_term = dot(q_buf[...], g_buf[...], ((1,), (1,)))
+    for i in range(nx):
+        h_loc[i] = h_term[:, i * pair : (i + 1) * pair]
     h_sib_copy = send(h_loc, h_sib, h_sib_sems, "tensor", sibling)
     h_sib_copy.wait_recv()
     h_chip[...] = h_loc[...] + h_sib[...]
     h_copies = [
-        send(h_chip, h_x.at[d], h_x_sems.at[d], "tensor", x_peer(d)) for d in range(1, nx)
-    ]
-
-    a_fwd = []
-    for p in range(pieces):
-        for d in range(1, nx):
-            a_x[d, p].wait_recv()
-            rows = token_rows(x_source(d), p)
-            a_fwd.append(
-                send(a_buf.at[rows], a_buf.at[rows], a_fwd_sems.at[d, :, p], "tensor", sibling)
-            )
-    h_sum = h_chip[...]
-    for d, copy in zip(range(1, nx), h_copies):
-        copy.wait_recv()
-        h_sum = h_sum + h_x[d]
+        send(
+            h_chip.at[lax.rem(chip + d, nx)], h_x.at[d], h_x_sems.at[d], "tensor", x_peer(d)
+        )
+        for d in range(1, nx)
+    ]
     loads[2].wait()
     a_sib.wait_recv()
-    for copy in a_fwd:
-        copy.wait_recv()
-    a_out = pltpu.make_async_copy(a_buf, acat_ref.at[pl.ds(0, tokens)], local_sems.at[3])
-    a_out.start()
+    h_sum = h_chip[chip]
+    for d, copy in zip(range(1, nx), h_copies):
+        copy.wait_recv()
+        h_sum = h_sum + h_x[d]
 
     h_both = jnp.concatenate(split(h_sum), axis=0)
-    own = dot(
-        h_both, a_buf[:, pl.ds(pl.multiple_of(t * part, part), part)], ((1,), (0,))
-    )
-    own = (own[:rank] + own[rank:]) * (1.0 / nd)
+    chip_rows = pl.ds(pl.multiple_of(chip * pair, pair), pair)
+
+    def p_rows(owner):
+        columns = pl.ds(pl.multiple_of(owner * part, part), part)
+        both = dot(h_both, a_buf[chip_rows, columns], ((1,), (0,)))
+        return (both[:rank] + both[rank:]) * (1.0 / nd)
+
+    ptok = []
+    for d in range(1, nx):
+        p_here[d] = p_rows(x_peer(d))
+        ptok.append(send(p_here.at[d], p_there.at[d], ptok_sems.at[d], "tensor", x_peer(d)))
+    own = p_rows(t)
+    for d, copy in zip(range(1, nx), ptok):
+        copy.wait_recv()
+        own = own + p_there[d]
+    late = max(early, pieces - pieces // 4)
+    send_tokens(early, late)
     for j in range(nd):
         p_part[j] = own[:, j * chunk : (j + 1) * chunk]
     copies = [
         send(p_part.at[z_peer(d)], p_recv.at[d], prs_sems.at[d], "dp", z_peer(d))
         for d in range(1, nd)
     ]
+    forward_tokens(0, early)
     total = p_part[z]
     for d, copy in zip(range(1, nd), copies):
         copy.wait_recv()
@@ -182,11 +206,13 @@
         for e in range(1, nx):
             px[e, d] = send(block, block, px_sems.at[e, :, d], "tensor", x_peer(e))
         psib.append(send(block, block, psib_sems.at[:, d], "tensor", sibling))
+    send_tokens(late, pieces)
     for d in range(nd):
         for e in range(1, nx):
             px[e, d].wait_recv()
             block = p_all.at[x_source(e), z_source(d)]
             pfwd.append(send(block, block, pfwd_sems.at[e, :, d], "tensor", sibling))
+    forward_tokens(early, late)
     for copy in psib + pfwd:
         copy.wait_recv()
     for i in range(nt):
@@ -196,14 +222,43 @@
 
     gram = dot(p_t[...], p_t[...], ((1,), (1,)), HIGHEST)
     inverse = inverse_factor(gram)
+    forward_tokens(late, pieces)
     p_orth = dot(inverse, p_t[...], ((1,), (0,)), HIGHEST)
     p_high, p_rest = split(p_orth)
     p_neg[0:rank] = -p_high
     p_neg[rank : 2 * rank] = -p_rest
     p_out = pltpu.make_async_copy(
-        p_neg, acat_ref.at[pl.ds(tokens, 2 * rank)], local_sems.at[4]
+        p_neg, pneg_ref, local_sems.at[4]
     )
     p_out.start()
+
+    for copy in a_fwd:
+        copy.wait_recv()
+
+    rows = stage.shape[1]
+    steps = depth // rows
+    width = g_buf.shape[1]
+    columns = 512 if width % 512 == 0 else 128
+
+    def write(slot, row):
+        return pltpu.make_async_copy(
+            stage.at[slot], merged_ref.at[pl.ds(row, rows)], stage_sems.at[slot]
+        )
+
+    def merge(i, _):
+        slot = lax.rem(i, 2)
+        row = pl.multiple_of(i * rows, rows)
+
+        @pl.when(i >= 2)
+        def _():
+            write(slot, row).wait()
+
+        lhs = a_buf[:, pl.ds(row, rows)].T
+        for j in range(width // columns):
+            cols = slice(j * columns, (j + 1) * columns)
+            stage[slot, :, cols] = dot(lhs, g_buf[:, cols], ((1,), (0,))).astype(BF16)
+        write(slot, row).start()
+        return 0
 
     u_both = jnp.concatenate(split(dot(p_high, a_buf[...], ((1,), (1,)))), axis=0)
     term = dot(u_both, g_buf[...], ((1,), (0,)))
@@ -215,6 +270,7 @@
         send(q_part.at[z_peer(d)], q_recv.at[d], qrs_sems.at[d], "dp", z_peer(d))
         for d in range(1, nd)
     ]
+    lax.fori_loop(0, steps // 2, merge, 0)
     total = q_f32[pl.ds(pl.multiple_of(z * q_rows, q_rows), q_rows), :]
     for d, copy in zip(range(1, nd), copies):
         copy.wait_recv()
@@ -223,23 +279,26 @@
     copies = [
         send(q_all.at[z], q_all.at[z], qag_sems.at[d], "dp", z_peer(d)) for d in range(1, nd)
     ]
+    lax.fori_loop(steps // 2, steps, merge, 0)
     for copy in copies:
         copy.wait_recv()
     q_out = pltpu.make_async_copy(q_all, qnew_ref, local_sems.at[5])
     q_out.start()
     for copy in pending:
         copy.wait_send()
-    a_out.wait()
+    for slot in range(2):
+        write(slot, 0).wait()
     p_out.wait()
     q_out.wait()
 
 
-def factors(nt, nd, activations, out_grads, q_start):
+def factors(nt, nd, activations, out_grads, q_t):
     tok, depth = activations.shape[1:]
     tokens, width = out_grads.shape[1:]
-    rank = q_start.shape[1]
+    rank = q_t.shape[0]
     nx = nt // 2
-    pieces = 2
+    pair = 2 * tok
+    pieces = min(4, tok // 16)
     part = depth // nt
     chunk = part // nd
     q_rows = rank // nd
@@ -249,19 +308,22 @@
     return pl.pallas_call(
         functools.partial(factors_kernel, nt, nd),
         out_shape=(
-            jax.ShapeDtypeStruct((tokens + 2 * rank, depth), BF16),
+            jax.ShapeDtypeStruct((depth, width), BF16),
+            jax.ShapeDtypeStruct((2 * rank, depth), BF16),
             jax.ShapeDtypeStruct((nd, q_rows, width), q_type),
         ),
         in_specs=[anywhere] * 3,
-        out_specs=(anywhere, anywhere),
+        out_specs=(anywhere, anywhere, anywhere),
         scratch_shapes=[
             pltpu.VMEM((tokens, depth), BF16),
             pltpu.VMEM((tokens, width), BF16),
-            pltpu.VMEM((width, rank), BF16),
-            pltpu.VMEM((rank, tokens), F32),
-            pltpu.VMEM((rank, tokens), F32),
-            pltpu.VMEM((rank, tokens), F32),
-            pltpu.VMEM((nx, rank, tokens), F32),
+            pltpu.VMEM((rank, width), BF16),
+            pltpu.VMEM((nx, rank, pair), F32),
+            pltpu.VMEM((nx, rank, pair), F32),
+            pltpu.VMEM((nx, rank, pair), F32),
+            pltpu.VMEM((nx, rank, pair), F32),
+            pltpu.VMEM((nx, rank, part), F32),
+            pltpu.VMEM((nx, rank, part), F32),
             pltpu.VMEM((nd, rank, chunk), F32),
             pltpu.VMEM((nd, rank, chunk), F32),
             pltpu.VMEM((nt, nd, rank, chunk), F32),
@@ -271,11 +333,14 @@
             pltpu.VMEM((nd, q_rows, width), q_type),
             pltpu.VMEM((nd, q_rows, width), q_type),
             pltpu.VMEM((nd, q_rows, width), q_type),
+            pltpu.VMEM((2, 512, width), BF16),
             dma((6,)),
+            dma((2,)),
             dma((2,)),
             dma((nx, 2, pieces)),
             dma((nx, 2, pieces)),
             dma((2,)),
+            dma((nx, 2)),
             dma((nx, 2)),
             dma((nd, 2)),
             dma((nd, 2)),
@@ -286,43 +351,40 @@
             dma((nd, 2)),
         ],
         compiler_params=pltpu.CompilerParams(
-            collective_id=0, has_side_effects=True, vmem_limit_bytes=48 * 2**20
+            collective_id=0, has_side_effects=True, vmem_limit_bytes=61 * 2**20
         ),
         name="factors",
-    )(activations, out_grads, q_start)
-
-
-def finish_kernel(own, z_ref, acat_ref, g_ref, q_ref, wu_ref, qnew_ref, err_ref, lhs, both):
+    )(activations, out_grads, q_t)
+
+
+def finish_kernel(own, z_ref, merged_ref, pneg_ref, q_ref, wu_ref, qnew_ref, err_ref, lhs, both):
     step = pl.program_id(0)
-    tokens, width = g_ref.shape[1:]
+    width = merged_ref.shape[1]
     rank = q_ref.shape[0]
-    lhs[...] = acat_ref[...].T
+    lhs[...] = pneg_ref[...].T
 
     @pl.when(step == 0)
     def _():
         both[0:rank] = q_ref[...].astype(BF16)
         both[rank : 2 * rank] = q_ref[...].astype(BF16)
-        qnew_ref[...] = q_ref[...].astype(F32).T
+        qnew_ref[...] = q_ref[...].astype(F32)
 
     columns = 512 if width % 512 == 0 else 128
-    for j in range(width // columns):
-        cols = slice(j * columns, (j + 1) * columns)
-        minus = dot(lhs[:, tokens:], both[:, cols], ((1,), (0,)))
-        err_ref[0, :, cols] = (
-            dot(lhs[:, :tokens], g_ref[0, :, cols], ((1,), (0,))) + minus
-        ).astype(BF16)
-
-    @pl.when(step < own)
-    def _():
+
+    def tiles(update):
         for j in range(width // columns):
             cols = slice(j * columns, (j + 1) * columns)
-            minus = dot(lhs[:, tokens:], both[:, cols], ((1,), (0,)))
-            wu_ref[:, cols] = (-minus).astype(BF16)
-
-
-def finish(nd, acat, out_grads, q_t):
-    depth = acat.shape[1]
-    tokens, width = out_grads.shape[1:]
+            minus = dot(lhs[...], both[:, cols], ((1,), (0,)))
+            err_ref[0, :, cols] = (merged_ref[:, cols].astype(F32) + minus).astype(BF16)
+            if update:
+                wu_ref[:, cols] = (-minus).astype(BF16)
+
+    pl.when(step < own)(lambda: tiles(True))
+    pl.when(step >= own)(lambda: tiles(False))
+
+
+def finish(nd, merged, p_neg, q_t):
+    depth, width = merged.shape
     rank = q_t.shape[0]
     rows = 256
     steps = depth // rows
@@ -336,38 +398,39 @@
         functools.partial(finish_kernel, own),
         out_shape=(
             jax.ShapeDtypeStruct((depth // nd, width), BF16),
-            jax.ShapeDtypeStruct((width, rank), F32),
+            jax.ShapeDtypeStruct((rank, width), F32),
             jax.ShapeDtypeStruct((1, depth, width), BF16),
         ),
         grid_spec=pltpu.PrefetchScalarGridSpec(
             num_scalar_prefetch=1,
             grid=(steps,),
             in_specs=[
-                pl.BlockSpec((acat.shape[0], rows), lambda i, z: (0, at(i, z))),
-                pl.BlockSpec((1, tokens, width), lambda i, z: (0, 0, 0)),
+                pl.BlockSpec((rows, width), lambda i, z: (at(i, z), 0)),
+                pl.BlockSpec((2 * rank, rows), lambda i, z: (0, at(i, z))),
                 pl.BlockSpec((rank, width), lambda i, z: (0, 0)),
             ],
             out_specs=(
                 pl.BlockSpec((rows, width), lambda i, z: (jnp.minimum(i, own - 1), 0)),
-                pl.BlockSpec((width, rank), lambda i, z: (0, 0)),
+                pl.BlockSpec((rank, width), lambda i, z: (0, 0)),
                 pl.BlockSpec((1, rows, width), lambda i, z: (0, at(i, z), 0)),
             ),
             scratch_shapes=[
-                pltpu.VMEM((rows, acat.shape[0]), BF16),
+                pltpu.VMEM((rows, 2 * rank), BF16),
                 pltpu.VMEM((2 * rank, width), BF16),
             ],
         ),
         compiler_params=pltpu.CompilerParams(
-            dimension_semantics=("arbitrary",), vmem_limit_bytes=48 * 2**20
+            dimension_semantics=("arbitrary",), vmem_limit_bytes=30 * 2**20
         ),
         name="finish",
-    )(z, acat, out_grads, q_t)
+    )(z, merged, p_neg, q_t)
 
 
 def per_device(nt, nd, activations, out_grads, q_start):
-    acat, q_parts = factors(nt, nd, activations, out_grads, q_start)
+    merged, p_neg, q_parts = factors(nt, nd, activations, out_grads, q_start.T)
     q_t = q_parts.reshape(q_start.shape[1], out_grads.shape[2])
-    return finish(nd, acat, out_grads, q_t)
+    weight_update, q_new, new_error = finish(nd, merged, p_neg, q_t)
+    return weight_update, q_new.T, new_error
 
 
 def solution(mesh):

time: 125 us -> 106 us (0.85); the launches traced: 122 us -> 105 us
  Pallas kernels: 115 us -> 102 us
  local copies, waits for them, and re-layouts: 6.15 us -> 2.24 us
    pallas_call x1, Pallas kernels: 81.6 us -> 73.5 us  [factors(): pl.pallas_call(functools.partial(factors_kernel, nt, nd), out_shape=(jax....]
    pallas_call x1, Pallas kernels: 33.7 us -> 28.2 us  [finish(): pl.pallas_call(functools.partial(finish_kernel, own), out_shape=(jax.Shap...]
    unnamed x7 -> x4, local copies, waits for them, and re-layouts: 4.71 us -> 2.24 us
    pallas_call x1 -> x0, local copies, waits for them, and re-layouts: 1.44 us -> none  [finish(): pl.pallas_call(functools.partial(finish_kernel, own), out_shape=(jax.Shap...]
where the time goes in v2:
time: 106 us; the launch traced here: 105 us
  Pallas kernels  102 us (96%)
  local copies, waits for them, and re-layouts  2.24 us (2%)
    pallas_call x1, Pallas kernels, factors(): pl.pallas_call(functools.partial(factors_kernel, nt, nd), out_shape=(jax....  73.5 us
    pallas_call x1, Pallas kernels, finish(): pl.pallas_call(functools.partial(finish_kernel, own), out_shape=(jax.Shap...  28.2 us
    unnamed x4, local copies, waits for them, and re-layouts  2.24 us

profile of v2, /device:TPU:0, one launch (start us, length us, event | category | flops | bytes accessed | tf_op | source)
XLA Modules:
  0.0 104.6 jit_solution(17374759490479388432)
XLA Ops:
  0.6 73.5 %factors.1 = (bf16[4096,3584]{1,0:T(8,128)(2,1)}, bf16[128,4096]{1,0:T(8,128)(2,1)}, bf16[4,16,3584]{2,1,0:T(8,128)(2,1)}) custom-call(bf16[1,128,4096]{2,1,0:T(8,128)(2,1)} %a_ref.1, bf16[1,512,3584]{2,1,0:T(8,128)(2,1)} %g_ref.1, bf16[64,3584]{1,0:T(8,128)(2,1)} %bitcast.5), custom_call_target="tpu_custom_call" | custom-call | tf_op jit(solution)/shard_map/factors/pallas_call | solution.py:308
  74.2 0.0 copy-start
  74.2 1.2 %copy-done = bf16[128,4096]{1,0:T(8,128)(2,1)S(1)} copy-done((bf16[128,4096]{1,0:T(8,128)(2,1)S(1)}, bf16[128,4096]{1,0:T(8,128)(2,1)}, u32[]{:S(2)}) %copy-start) | copy-done | bytes 1048600
  75.4 0.0 copy-start.1
  75.4 1.0 copy-done.1
  76.4 28.2 %finish.1 = (bf16[1024,3584]{1,0:T(8,128)(2,1)}, f32[64,3584]{1,0:T(8,128)}, bf16[1,4096,3584]{2,1,0:T(8,128)(2,1)}) custom-call(s32[1]{0:T(128)} %bitcast.z_ref, bf16[4096,3584]{1,0:T(8,128)(2,1)} %get-tuple-element.9.merged_ref, bf16[128,4096]{1,0:T(8,128)(2,1)S(1)} %copy-done, bf16[64,3584]{1,0:T(8,128)(2,1)S(1)} %bitcast.4), custom_call_target="tpu_custom_call" | custom-call | tf_op jit(solution)/shard_map/finish/pallas_call | solution.py:397
Async XLA Ops:
  74.2 1.2 %copy-start = (bf16[128,4096]{1,0:T(8,128)(2,1)S(1)}, bf16[128,4096]{1,0:T(8,128)(2,1)}, u32[]{:S(2)}) copy-start(bf16[128,4096]{1,0:T(8,128)(2,1)} %get-tuple-element.10.pneg_ref) | copy-start | bytes 3145732
  75.4 1.0 copy-start.1

commit v3 on v2

--- a/solution.py
+++ b/solution.py
@@ -32,20 +32,20 @@
     eye = (lanes == rows + rank).astype(F32)
     wide = jnp.concatenate([gram, jnp.zeros_like(gram)], axis=1) + eye
     done = []
-    for k in range(rank):
-        top = (k // 8) * 8
-        here = k - top
-        column = jnp.broadcast_to(wide[:, k : k + 1], wide.shape)
-        pivot_row = wide[here : here + 1, :]
-        pivot = column[here : here + 1, :]
-        done.append(pivot_row * lax.rsqrt(pivot))
-        if k == rank - 1:
-            break
-        scaled = pivot_row / pivot
-        below = lax.broadcasted_iota(jnp.int32, wide.shape, 0) > here
-        wide = jnp.where(below, wide - column * scaled, wide)
-        if here == 7:
-            wide = wide[8:, :]
+    group = 8
+    for top in range(0, rank, group):
+        columns = [
+            jnp.broadcast_to(wide[:, top + i : top + i + 1], wide.shape) for i in range(group)
+        ]
+        for i in range(group):
+            pivot_row = wide[i : i + 1, :]
+            pivot = columns[i][i : i + 1, :]
+            inverse = 1.0 / pivot
+            done.append(pivot_row * lax.rsqrt(pivot))
+            wide = wide - columns[i] * (pivot_row * inverse)
+            for j in range(i + 1, group):
+                columns[j] = columns[j] - columns[i] * (columns[j][i : i + 1, :] * inverse)
+        wide = wide[group:, :]
     return jnp.concatenate(done, axis=0)[:, rank:]
 
 
@@ -308,9 +308,9 @@
     return pl.pallas_call(
         functools.partial(factors_kernel, nt, nd),
         out_shape=(
-            jax.ShapeDtypeStruct((depth, width), BF16),
-            jax.ShapeDtypeStruct((2 * rank, depth), BF16),
-            jax.ShapeDtypeStruct((nd, q_rows, width), q_type),
+            pltpu.VMEM((depth, width), BF16),
+            pltpu.VMEM((2 * rank, depth), BF16),
+            pltpu.VMEM((nd, q_rows, width), q_type),
         ),
         in_specs=[anywhere] * 3,
         out_specs=(anywhere, anywhere, anywhere),
@@ -351,7 +351,7 @@
             dma((nd, 2)),
         ],
         compiler_params=pltpu.CompilerParams(
-            collective_id=0, has_side_effects=True, vmem_limit_bytes=61 * 2**20
+            collective_id=0, has_side_effects=True, vmem_limit_bytes=34 * 2**20
         ),
         name="factors",
     )(activations, out_grads, q_t)
@@ -420,7 +420,7 @@
             ],
         ),
         compiler_params=pltpu.CompilerParams(
-            dimension_semantics=("arbitrary",), vmem_limit_bytes=30 * 2**20
+            dimension_semantics=("arbitrary",), vmem_limit_bytes=34 * 2**20
         ),
         name="finish",
     )(z, merged, p_neg, q_t)
@@ -429,6 +429,9 @@
 def per_device(nt, nd, activations, out_grads, q_start):
     merged, p_neg, q_parts = factors(nt, nd, activations, out_grads, q_start.T)
     q_t = q_parts.reshape(q_start.shape[1], out_grads.shape[2])
+    merged, p_neg, q_t = (
+        pltpu.with_memory_space_constraint(x, pltpu.VMEM) for x in (merged, p_neg, q_t)
+    )
     weight_update, q_new, new_error = finish(nd, merged, p_neg, q_t)
     return weight_update, q_new.T, new_error
 

time: 106 us -> 89.7 us (0.85)
  Pallas kernels: 102 us -> 87.7 us
  local copies, waits for them, and re-layouts: 2.24 us -> 0 us
    pallas_call x1, Pallas kernels: 28.2 us -> 18.4 us  [finish(): pl.pallas_call(functools.partial(finish_kernel, own), out_shape=(jax.Shap...]
    pallas_call x1, Pallas kernels: 73.5 us -> 69.3 us  [factors(): pl.pallas_call(functools.partial(factors_kernel, nt, nd), out_shape=(pltp...]
    unnamed x4 -> x0, local copies, waits for them, and re-layouts: 2.24 us -> none
where the time goes in v3:
time: 89.7 us; the launch traced here: 88.3 us
  Pallas kernels  87.7 us (98%)
    pallas_call x1, Pallas kernels, factors(): pl.pallas_call(functools.partial(factors_kernel, nt, nd), out_shape=(pltp...  69.3 us
    pallas_call x1, Pallas kernels, finish(): pl.pallas_call(functools.partial(finish_kernel, own), out_shape=(jax.Shap...  18.4 us

profile of v3, /device:TPU:0, one launch (start us, length us, event | category | flops | bytes accessed | tf_op | source)
XLA Modules:
  0.0 88.3 jit_solution(4802671278496541799)
XLA Ops:
  0.6 69.3 %factors.1 = (bf16[4096,3584]{1,0:T(8,128)(2,1)S(1)}, bf16[128,4096]{1,0:T(8,128)(2,1)S(1)}, bf16[4,16,3584]{2,1,0:T(8,128)(2,1)S(1)}) custom-call(bf16[1,128,4096]{2,1,0:T(8,128)(2,1)} %a_ref.1, bf16[1,512,3584]{2,1,0:T(8,128)(2,1)} %g_ref.1, bf16[64,3584]{1,0:T(8,128)(2,1)} %bitcast.5), custom_call_target="tpu_custom_call" | custom-call | tf_op jit(solution)/shard_map/factors/pallas_call | solution.py:308
  69.9 18.4 %finish.1 = (bf16[1024,3584]{1,0:T(8,128)(2,1)}, f32[64,3584]{1,0:T(8,128)}, bf16[1,4096,3584]{2,1,0:T(8,128)(2,1)}) custom-call(s32[1]{0:T(128)} %bitcast.z_ref, bf16[4096,3584]{1,0:T(8,128)(2,1)S(1)} %get-tuple-element.9.merged_ref, bf16[128,4096]{1,0:T(8,128)(2,1)S(1)} %get-tuple-element.10.pneg_ref, bf16[64,3584]{1,0:T(8,128)(2,1)S(1)} %bitcast.4), custom_call_target="tpu_custom_call" | custom-call | tf_op jit(solution)/shard_map/finish/pallas_call | solution.py:397

commit v4 on v3

--- a/solution.py
+++ b/solution.py
@@ -180,7 +180,7 @@
     for d, copy in zip(range(1, nx), ptok):
         copy.wait_recv()
         own = own + p_there[d]
-    late = max(early, pieces - pieces // 4)
+    late = early + (pieces - early) // 3
     send_tokens(early, late)
     for j in range(nd):
         p_part[j] = own[:, j * chunk : (j + 1) * chunk]
@@ -370,12 +370,15 @@
         qnew_ref[...] = q_ref[...].astype(F32)
 
     columns = 512 if width % 512 == 0 else 128
+    rows = err_ref.shape[1]
+    block = lax.rem(step + z_ref[0] * own, pl.num_programs(0))
+    here = pl.ds(pl.multiple_of(block * rows, rows), rows)
 
     def tiles(update):
         for j in range(width // columns):
             cols = slice(j * columns, (j + 1) * columns)
             minus = dot(lhs[...], both[:, cols], ((1,), (0,)))
-            err_ref[0, :, cols] = (merged_ref[:, cols].astype(F32) + minus).astype(BF16)
+            err_ref[0, :, cols] = (merged_ref[here, cols].astype(F32) + minus).astype(BF16)
             if update:
                 wu_ref[:, cols] = (-minus).astype(BF16)
 
@@ -405,7 +408,7 @@
             num_scalar_prefetch=1,
             grid=(steps,),
             in_specs=[
-                pl.BlockSpec((rows, width), lambda i, z: (at(i, z), 0)),
+                pl.BlockSpec(memory_space=pltpu.VMEM),
                 pl.BlockSpec((2 * rank, rows), lambda i, z: (0, at(i, z))),
                 pl.BlockSpec((rank, width), lambda i, z: (0, 0)),
             ],

time: 89.7 us -> 91.1 us (1.016); the launches traced: 88.3 us -> 91 us
  Pallas kernels: 87.7 us -> 90.3 us
    pallas_call x1, Pallas kernels: 69.3 us -> 71.9 us  [factors(): pl.pallas_call(functools.partial(factors_kernel, nt, nd), out_shape=(pltp...]
where the time goes in v4:
time: 91.1 us; the launch traced here: 91 us
  Pallas kernels  90.3 us (99%)
    pallas_call x1, Pallas kernels, factors(): pl.pallas_call(functools.partial(factors_kernel, nt, nd), out_shape=(pltp...  71.9 us
    pallas_call x1, Pallas kernels, finish(): pl.pallas_call(functools.partial(finish_kernel, own), out_shape=(jax.Shap...  18.4 us

profile of v4, /device:TPU:0, one launch (start us, length us, event | category | flops | bytes accessed | tf_op | source)
XLA Modules:
  0.0 91.0 jit_solution(18099218512138012823)
XLA Ops:
  0.6 71.9 %factors.1 = (bf16[4096,3584]{1,0:T(8,128)(2,1)S(1)}, bf16[128,4096]{1,0:T(8,128)(2,1)S(1)}, bf16[4,16,3584]{2,1,0:T(8,128)(2,1)S(1)}) custom-call(bf16[1,128,4096]{2,1,0:T(8,128)(2,1)} %a_ref.1, bf16[1,512,3584]{2,1,0:T(8,128)(2,1)} %g_ref.1, bf16[64,3584]{1,0:T(8,128)(2,1)} %bitcast.5), custom_call_target="tpu_custom_call" | custom-call | tf_op jit(solution)/shard_map/factors/pallas_call | solution.py:308
  72.6 18.4 %finish.1 = (bf16[1024,3584]{1,0:T(8,128)(2,1)}, f32[64,3584]{1,0:T(8,128)}, bf16[1,4096,3584]{2,1,0:T(8,128)(2,1)}) custom-call(s32[1]{0:T(128)} %bitcast.z_ref, bf16[4096,3584]{1,0:T(8,128)(2,1)S(1)} %get-tuple-element.9.merged_ref, bf16[128,4096]{1,0:T(8,128)(2,1)S(1)} %get-tuple-element.10.pneg_ref, bf16[64,3584]{1,0:T(8,128)(2,1)S(1)} %bitcast.4), custom_call_target="tpu_custom_call" | custom-call | tf_op jit(solution)/shard_map/finish/pallas_call | solution.py:400
